TPU v7x, 32 devices: a whole 2x2x4 slice. The times are simulated.
32 devices in a mesh: groups: 2 (over y), locus: 4 (over z), design: 2 (over x), chan: 2 (over core).
Axes of the slice: x: 2, y: 2, z: 4, core: 2. Of those that a mesh axis runs over, the one named last changes fastest.
Arguments:
- base_seq: bfloat16 [4, 2048, 128], P(('groups', 'design'), 'locus'), parts along dimension 0, may hold values from -6 to 6
- deltas: bfloat16 [2048, 512], P(('groups', 'locus', 'design')), parts along dimension 0, may hold values from -6 to 6
- owners: int32 [2048, 1], P(('groups', 'locus', 'design')), parts along dimension 0, may hold values from 0 to 7; in each aligned block of 128 rows (0 to 127, 128 to 255, ...) at most 32 rows name the same one
- slot_ids: int32 [2048], P(('groups', 'locus', 'design')), parts along dimension 0, may hold values from 0 to 127
- stem_weight: bfloat16 [128, 1536], P(None, 'chan'), may hold values from -0.5 to 0.5
- dilated_tap_weight: bfloat16 [3, 1536, 768], P(None, None, 'chan'), may hold values from -0.09375 to 0.09375
- mix_weight: bfloat16 [768, 1536], P('chan'), may hold values from -0.21875 to 0.21875
- head_weight: bfloat16 [1536], replicated, may hold values from -5 to 5
Outputs:
- window_grad: float32 [2048, 512], P(('groups', 'locus', 'design')), parts along dimension 0
There are 2 independent parts, one for each index of `groups`. A program takes and returns all parts, laid end to end along the dimension named above; an argument that names none is the same for every part. Nothing has to cross between parts.
Inputs may be any that keep to these rules, and one draw needn't show every extreme that they name: `owners`: owner o stands for bins of segment o // 2 of locus o % 2. Among the 128 windows of one device no owner is named more than 32 times, a bound that some block reaches. `slot_ids`: several windows may name the same target; their changes add.
All inputs are finite; a program needn't handle non-finite values.
Results may differ from a plain program's by a relative error of at most 0.0055.
Values may be sent and summed in bfloat16 or wider, within the bound.
A program may use at most 64 MiB of HBM per device.

v0:
```python
import jax
import jax.numpy as jnp
from jax import lax
from jax.sharding import PartitionSpec as P

DILATION_STEP = 32


def with_halo(cells, sides, width):
    for axis, dim in sides:
        count = lax.axis_size(axis)
        ends = count - 1
        head = lax.slice_in_dim(cells, 0, width, axis=dim)
        tail = lax.slice_in_dim(cells, cells.shape[dim] - width, cells.shape[dim], axis=dim)
        cells = jnp.concatenate(
            [
                lax.ppermute(tail, axis, [(i, (i + 1) % count) for i in range(ends)]),
                cells,
                lax.ppermute(head, axis, [((i + 1) % count, i) for i in range(ends)]),
            ],
            axis=dim,
        )
    return cells


def silu_slope(pre_value):
    sigmoid_value = jax.nn.sigmoid(pre_value)
    return sigmoid_value * (1.0 + pre_value * (1.0 - sigmoid_value))


def gelu_pull(pre_act, cotangent):
    return jax.vjp(lambda argument: jax.nn.gelu(argument, approximate=True), pre_act)[1](cotangent)[
        0
    ]


def stem_back(pulled, weight):
    upper = pulled.astype(jnp.bfloat16)
    lower = (pulled - upper.astype(jnp.float32)).astype(jnp.bfloat16)
    dims = (((1,), (1,)), ((), ()))
    first = lax.dot_general(upper, weight, dims, preferred_element_type=jnp.float32)
    return first + lax.dot_general(lower, weight, dims, preferred_element_type=jnp.float32)


def shards(
    base_seq, deltas, owners, slot_ids, stem_weight, dilated_tap_weight, mix_weight, head_weight
):
    win_dev, row_width = deltas.shape
    bins_per_device, feat_width = (base_seq.shape[1], base_seq.shape[2])
    slots_dev = bins_per_device * feat_width // row_width
    peer_count = lax.axis_size(("locus", "design"))
    capacity = max(2, 2 * win_dev // peer_count)
    bucket_rows = peer_count * capacity
    target_dev = owners[:, 0]
    member = (target_dev[:, None] == jnp.arange(peer_count, dtype=jnp.int32)[None, :]).astype(
        jnp.int32
    )
    earlier = jnp.cumsum(member, axis=0) - member
    bucket_rank = jnp.sum(earlier * member, axis=1)
    position = target_dev * capacity + bucket_rank
    placer = position[None, :] == jnp.arange(bucket_rows, dtype=jnp.int32)[:, None]
    send_rows = jnp.dot(
        placer.astype(jnp.bfloat16), deltas, preferred_element_type=jnp.float32
    ).astype(jnp.bfloat16)
    send_slots = jnp.sum(jnp.where(placer, slot_ids[None, :], 0), axis=1)
    recv_rows, recv_slots = (
        lax.all_to_all(send_rows, ("locus", "design"), split_axis=0, concat_axis=0, tiled=True),
        lax.all_to_all(send_slots, ("locus", "design"), split_axis=0, concat_axis=0, tiled=True),
    )
    chooser = recv_slots[:, None] == jnp.arange(slots_dev, dtype=jnp.int32)[None, :]
    edit_sum = lax.dot_general(
        chooser.astype(jnp.bfloat16),
        recv_rows,
        (((0,), (0,)), ((), ())),
        preferred_element_type=jnp.float32,
    )
    sequence_onehot = (
        base_seq[0].astype(jnp.float32) + edit_sum.reshape(bins_per_device, feat_width)
    ).astype(jnp.bfloat16)
    padded_sequence = with_halo(sequence_onehot, (("locus", 0),), DILATION_STEP)
    stem_full = lax.all_gather(stem_weight, "chan", axis=1, tiled=True)
    gathered_preactivation = jnp.dot(padded_sequence, stem_full, preferred_element_type=jnp.float32)
    hidden_state = jax.nn.gelu(gathered_preactivation, approximate=True).astype(jnp.bfloat16)
    own_width = dilated_tap_weight.shape[2]
    convolved_output = jnp.zeros((bins_per_device, own_width), jnp.float32)
    for filter_tap in range(3):
        convolved_output = convolved_output + jnp.dot(
            hidden_state[filter_tap * DILATION_STEP : filter_tap * DILATION_STEP + bins_per_device],
            dilated_tap_weight[filter_tap],
            preferred_element_type=jnp.float32,
        )
    mix_grad = jnp.dot(mix_weight, head_weight, preferred_element_type=jnp.float32)
    residual_branch = (silu_slope(convolved_output) * mix_grad[None, :]).astype(jnp.bfloat16)
    padded_gradient = with_halo(residual_branch, (("locus", 0),), DILATION_STEP)
    part_sum = jnp.zeros((bins_per_device, stem_full.shape[1]), jnp.float32)
    for filter_tap in range(3):
        lower_boundary = (2 - filter_tap) * DILATION_STEP
        part_sum = part_sum + lax.dot_general(
            padded_gradient[lower_boundary : lower_boundary + bins_per_device],
            dilated_tap_weight[filter_tap],
            (((1,), (1,)), ((), ())),
            preferred_element_type=jnp.float32,
        )
    local_preactivation = gathered_preactivation[DILATION_STEP : DILATION_STEP + bins_per_device]
    summed = lax.psum(part_sum, "chan")
    hidden_grad = head_weight.astype(jnp.float32)[None, :] + summed
    pulled = gelu_pull(local_preactivation, hidden_grad)
    seq_grad = stem_back(pulled, stem_full)
    slot_grad = seq_grad.reshape(slots_dev, row_width)
    back_rows = jnp.dot(chooser.astype(jnp.float32), slot_grad, precision=lax.Precision.HIGHEST)
    returned = lax.all_to_all(
        back_rows, ("locus", "design"), split_axis=0, concat_axis=0, tiled=True
    )
    return lax.dot_general(
        placer.astype(jnp.float32),
        returned,
        (((0,), (0,)), ((), ())),
        precision=lax.Precision.HIGHEST,
    )


def solution(mesh):
    placed = (
        P(("groups", "design"), "locus", None),
        P(("groups", "locus", "design"), None),
        P(("groups", "locus", "design"), None),
        P(("groups", "locus", "design")),
        P(None, "chan"),
        P(None, None, "chan"),
        P("chan", None),
        P(),
    )
    return jax.shard_map(
        shards,
        mesh=mesh,
        in_specs=placed,
        out_specs=P(("groups", "locus", "design"), None),
        check_vma=False,
    )
```

profile of v0, /device:TPU:0, one launch (start us, length us, event | category | flops | bytes accessed | tf_op | source)
XLA Modules:
  0.0 118.4 jit_solution(7377365366886210995)
XLA Ops:
  6.5 0.8 fusion.66
  7.6 0.8 select_reduce_fusion.1
  8.4 0.7 multiply_add_fusion
  9.1 0.8 select_reduce_fusion
  9.8 0.7 all_to_all.22
  10.5 7.3 %all-to-all-start = ((s32[8,32,1]{1,2,0:T(1,128)}), s32[8,32,1]{1,2,0:T(1,128)S(1)}, u32[]{:S(2)}, u32[]{:S(2)}) async-start(s32[8,32,1]{1,2,0:T(1,128)} %all_to_all.22), calls=%async_computation | async-start | bytes 8192 | tf_op jit(solution)/shard_map/all_to_all | solution.py:68
  17.8 1.8 %convolution_convert_fusion = bf16[256,512]{1,0:T(8,128)(2,1)} fusion(bf16[128,512]{1,0:T(8,128)(2,1)} %param.9, s32[128]{0:T(128)S(1)} %multiply_add_fusion), kind=kOutput, calls=%fused_computation.29 | convolution fusion | flops 33718272 | bytes 393728 | tf_op jit(solution)/shard_map/dot_general | solution.py:62
  19.6 4.6 %all-to-all-done = s32[8,32,1]{1,2,0:T(1,128)S(1)} async-done(((s32[8,32,1]{1,2,0:T(1,128)}), s32[8,32,1]{1,2,0:T(1,128)S(1)}, u32[]{:S(2)}, u32[]{:S(2)}) %all-to-all-start) | async-done | bytes 1056 | tf_op jit(solution)/shard_map/all_to_all | solution.py:68
  24.2 3.4 %all-to-all-start.1 = ((bf16[8,32,512]{2,1,0:T(8,128)(2,1)}), bf16[8,32,512]{2,1,0:T(8,128)(2,1)S(1)}, u32[]{:S(2)}, u32[]{:S(2)}) async-start(bf16[8,32,512]{2,1,0:T(8,128)(2,1)} %bitcast.4), calls=%async_computation.1 | async-start | bytes 524288 | tf_op jit(solution)/shard_map/all_to_all | solution.py:67
  27.7 0.7 reshape.52
  29.4 0.6 reduce.5
  30.1 5.7 %all-to-all-done.1 = bf16[8,32,512]{2,1,0:T(8,128)(2,1)S(1)} async-done(((bf16[8,32,512]{2,1,0:T(8,128)(2,1)}), bf16[8,32,512]{2,1,0:T(8,128)(2,1)S(1)}, u32[]{:S(2)}, u32[]{:S(2)}) %all-to-all-start.1) | async-done | bytes 262176 | tf_op jit(solution)/shard_map/all_to_all | solution.py:67
  36.2 2.0 %collective-permute-start = (bf16[32,128]{1,0:T(8,128)(2,1)S(1)}, bf16[32,128]{1,0:T(8,128)(2,1)S(1)}, u32[]{:S(2)}, u32[]{:S(2)}) collective-permute-start(bf16[32,128]{1,0:T(8,128)(2,1)S(1)} %get-tuple-element.7), channel_id=1, source_target_pairs={{0,4},{4,8},{8,12},{1,5},{5,9},{9,13},{2,6},{6,10},{10,14},{3,7},{... | collective-permute-start | bytes 24584 | tf_op jit(solution)/shard_map/ppermute | solution.py:17
  38.2 1.3 %collective-permute-start.1 = (bf16[32,128]{1,0:T(8,128)(2,1)S(1)}, bf16[32,128]{1,0:T(8,128)(2,1)S(1)}, u32[]{:S(2)}, u32[]{:S(2)}) collective-permute-start(bf16[32,128]{1,0:T(8,128)(2,1)S(1)} %get-tuple-element.8), channel_id=1, source_target_pairs={{4,0},{8,4},{12,8},{5,1},{9,5},{13,9},{6,2},{10,6},{14,10},{7,3},{... | collective-permute-start | bytes 24584 | tf_op jit(solution)/shard_map/ppermute | solution.py:19
  39.5 2.1 %all_gather.3 = bf16[128,1536]{1,0:T(8,128)(2,1)S(1)} all-gather(bf16[128,768]{1,0:T(8,128)(2,1)S(1)} %copy-done.2), channel_id=1, replica_groups=mesh['groups'=2,'locus'=4,'design'=2,'chan'=2] {'chan'}, dimensions={1}, use_global_device_ids=true | all-gather | bytes 589824 | tf_op jit(solution)/shard_map/all_gather | solution.py:81
  41.6 2.1 %collective-permute-done.1 = bf16[32,128]{1,0:T(8,128)(2,1)S(1)} collective-permute-done((bf16[32,128]{1,0:T(8,128)(2,1)S(1)}, bf16[32,128]{1,0:T(8,128)(2,1)S(1)}, u32[]{:S(2)}, u32[]{:S(2)}) %collective-permute-start.1) | collective-permute-done | bytes 8224 | tf_op jit(solution)/shard_map/ppermute | solution.py:19
  43.8 2.9 %fusion.7 = (bf16[576,1536]{1,0:T(8,128)(2,1)S(1)}, f32[576,1536]{1,0:T(8,128)}) fusion(bf16[128,1536]{1,0:T(8,128)(2,1)S(1)} %all_gather.3, bf16[32,128]{1,0:T(8,128)(2,1)S(1)} %collective-permute-done.1, bf16[512,128]{1,0:T(8,128)(2,1)S(1)} %fusion.50, bf16[32,128]{1,0:T(8,128)(2,1)S(1)} %collective-permute-done), kind=kOutput, calls=%fused_computation.10 | convolution fusion | flops 234897408 | bytes 5849088 | tf_op jit(solution)/shard_map/dot_general | solution.py:82
  46.7 1.0 fusion.18
  47.7 1.0 fusion.22
  48.7 1.2 multiply_convert_fusion
  49.9 2.9 %collective-permute-start.3 = (bf16[32,384]{1,0:T(8,128)(2,1)S(1)}, bf16[32,384]{1,0:T(8,128)(2,1)S(1)}, u32[]{:S(2)}, u32[]{:S(2)}) collective-permute-start(bf16[32,384]{1,0:T(8,128)(2,1)S(1)} %get-tuple-element.6), channel_id=1, source_target_pairs={{0,4},{4,8},{8,12},{1,5},{5,9},{9,13},{2,6},{6,10},{10,14},{3,7},{... | collective-permute-start | bytes 73736 | tf_op jit(solution)/shard_map/ppermute | solution.py:17
  52.8 1.0 fusion.31
  53.8 1.3 %collective-permute-start.2 = (bf16[32,384]{1,0:T(8,128)(2,1)S(1)}, bf16[32,384]{1,0:T(8,128)(2,1)S(1)}, u32[]{:S(2)}, u32[]{:S(2)}) collective-permute-start(bf16[32,384]{1,0:T(8,128)(2,1)S(1)} %get-tuple-element.5), channel_id=1, source_target_pairs={{4,0},{8,4},{12,8},{5,1},{9,5},{13,9},{6,2},{10,6},{14,10},{7,3},{... | collective-permute-start | bytes 73736 | tf_op jit(solution)/shard_map/ppermute | solution.py:19
  55.1 1.0 fusion.28
  56.1 3.4 %collective-permute-done.2 = bf16[32,384]{1,0:T(8,128)(2,1)S(1)} collective-permute-done((bf16[32,384]{1,0:T(8,128)(2,1)S(1)}, bf16[32,384]{1,0:T(8,128)(2,1)S(1)}, u32[]{:S(2)}, u32[]{:S(2)}) %collective-permute-start.2) | collective-permute-done | bytes 24608 | tf_op jit(solution)/shard_map/ppermute | solution.py:19
  59.5 2.8 %fusion.8 = f32[512,1536]{1,0:T(8,128)} fusion(f32[512,1536]{1,0:T(8,128)S(1)} %fusion.28, f32[512,1536]{1,0:T(8,128)S(1)} %fusion.31, bf16[3,1536,384]{2,1,0:T(8,128)(2,1)S(1)} %copy-done.1, bf16[32,384]{1,0:T(8,128)(2,1)S(1)} %collective-permute-done.2, bf16[512,384]{1,0:T(8,128)(2,1)S(1)} %multiply_convert_fusion), kind=kOutput, calls=%fused_computation.12 | convolution fusion | flops 606339072 | bytes 11034624 | tf_op jit(solution)/shard_map/dot_general | solution.py:98
  62.3 0.7 copy-done.4
  63.0 21.2 %all-reduce.2.cloned.1.call-done = f32[512,1536]{1,0:T(8,128)} async-done(((f32[512,1536]{1,0:T(8,128)}), f32[512,1536]{1,0:T(8,128)}) %all-reduce.2.cloned.1.call-update) | async-done | bytes 3145744 | tf_op jit(solution)/shard_map/psum | solution.py:105
  84.2 4.1 %fusion.14 = f32[512,1536]{1,0:T(8,128)S(1)} fusion(f32[576,1536]{1,0:T(8,128)} %get-tuple-element.10, f32[512,1536]{1,0:T(8,128)} %all-reduce.2.cloned.1.call-done, f32[1536]{0:T(1024)S(1)} %convert_element_type.38), kind=kLoop, calls=%fused_computation.18 | loop fusion | flops 15728640 | bytes 9443328 | tf_op jit(solution)/shard_map/transpose(jvp())/add_any | solution.py:32
  88.9 0.6 convolution_add_fusion.1
  89.9 20.5 %all_to_all.33 = f32[8,32,512]{2,1,0:T(8,128)S(1)} all-to-all(f32[8,32,512]{2,1,0:T(8,128)S(1)} %fusion.59), channel_id=1, replica_groups=mesh['groups'=2,'locus'=4,'design'=2,'chan'=2] {'locus','design'}, dimensions={0} | all-to-all | bytes 1048576 | tf_op jit(solution)/shard_map/all_to_all | solution.py:111
  110.4 1.1 fusion.57
  (26 shorter events, 2.7 us)
Async XLA Ops:
  6.5 21.9 %copy-start = (bf16[384,1536]{1,0:T(8,128)(2,1)S(1)}, bf16[384,1536]{1,0:T(8,128)(2,1)}, u32[]{:S(2)}) copy-start(bf16[384,1536]{1,0:T(8,128)(2,1)} %param.14) | copy-start | bytes 3538948
  6.5 29.6 %copy-start.3 = (bf16[1,512,128]{2,1,0:T(8,128)(2,1)S(1)}, bf16[1,512,128]{2,1,0:T(8,128)(2,1)}, u32[]{:S(2)}) copy-start(bf16[1,512,128]{2,1,0:T(8,128)(2,1)} %param.8) | copy-start | bytes 393220
  6.5 33.0 %copy-start.2 = (bf16[128,768]{1,0:T(8,128)(2,1)S(1)}, bf16[128,768]{1,0:T(8,128)(2,1)}, u32[]{:S(2)}) copy-start(bf16[128,768]{1,0:T(8,128)(2,1)} %param.12) | copy-start | bytes 589828
  10.5 13.7 %all-to-all-start = ((s32[8,32,1]{1,2,0:T(1,128)}), s32[8,32,1]{1,2,0:T(1,128)S(1)}, u32[]{:S(2)}, u32[]{:S(2)}) async-start(s32[8,32,1]{1,2,0:T(1,128)} %all_to_all.22), calls=%async_computation | async-start | bytes 8192 | tf_op jit(solution)/shard_map/all_to_all | solution.py:68
  24.2 11.6 %all-to-all-start.1 = ((bf16[8,32,512]{2,1,0:T(8,128)(2,1)}), bf16[8,32,512]{2,1,0:T(8,128)(2,1)S(1)}, u32[]{:S(2)}, u32[]{:S(2)}) async-start(bf16[8,32,512]{2,1,0:T(8,128)(2,1)} %bitcast.4), calls=%async_computation.1 | async-start | bytes 524288 | tf_op jit(solution)/shard_map/all_to_all | solution.py:67
  27.6 56.6 %all-reduce.2.cloned.1.call-start = ((), (), s32[]{:S(2)}) async-start(), calls=%async_computation.3 | async-start | bytes 6291456 | tf_op jit(solution)/shard_map/psum | solution.py:105
  36.2 5.4 %collective-permute-start = (bf16[32,128]{1,0:T(8,128)(2,1)S(1)}, bf16[32,128]{1,0:T(8,128)(2,1)S(1)}, u32[]{:S(2)}, u32[]{:S(2)}) collective-permute-start(bf16[32,128]{1,0:T(8,128)(2,1)S(1)} %get-tuple-element.7), channel_id=1, source_target_pairs={{0,4},{4,8},{8,12},{1,5},{5,9},{9,13},{2,6},{6,10},{10,14},{3,7},{... | collective-permute-start | bytes 24584 | tf_op jit(solution)/shard_map/ppermute | solution.py:17
  38.2 5.5 %collective-permute-start.1 = (bf16[32,128]{1,0:T(8,128)(2,1)S(1)}, bf16[32,128]{1,0:T(8,128)(2,1)S(1)}, u32[]{:S(2)}, u32[]{:S(2)}) collective-permute-start(bf16[32,128]{1,0:T(8,128)(2,1)S(1)} %get-tuple-element.8), channel_id=1, source_target_pairs={{4,0},{8,4},{12,8},{5,1},{9,5},{13,9},{6,2},{10,6},{14,10},{7,3},{... | collective-permute-start | bytes 24584 | tf_op jit(solution)/shard_map/ppermute | solution.py:19
  41.6 5.1 %copy-start.1 = (bf16[3,1536,384]{2,1,0:T(8,128)(2,1)S(1)}, bf16[3,1536,384]{2,1,0:T(8,128)(2,1)}, u32[]{:S(2)}) copy-start(bf16[3,1536,384]{2,1,0:T(8,128)(2,1)} %param.13) | copy-start | bytes 10616836
  49.9 5.3 %collective-permute-start.3 = (bf16[32,384]{1,0:T(8,128)(2,1)S(1)}, bf16[32,384]{1,0:T(8,128)(2,1)S(1)}, u32[]{:S(2)}, u32[]{:S(2)}) collective-permute-start(bf16[32,384]{1,0:T(8,128)(2,1)S(1)} %get-tuple-element.6), channel_id=1, source_target_pairs={{0,4},{4,8},{8,12},{1,5},{5,9},{9,13},{2,6},{6,10},{10,14},{3,7},{... | collective-permute-start | bytes 73736 | tf_op jit(solution)/shard_map/ppermute | solution.py:17
  53.8 5.7 %collective-permute-start.2 = (bf16[32,384]{1,0:T(8,128)(2,1)S(1)}, bf16[32,384]{1,0:T(8,128)(2,1)S(1)}, u32[]{:S(2)}, u32[]{:S(2)}) collective-permute-start(bf16[32,384]{1,0:T(8,128)(2,1)S(1)} %get-tuple-element.5), channel_id=1, source_target_pairs={{4,0},{8,4},{12,8},{5,1},{9,5},{13,9},{6,2},{10,6},{14,10},{7,3},{... | collective-permute-start | bytes 73736 | tf_op jit(solution)/shard_map/ppermute | solution.py:19
  62.3 0.7 copy-start.4
Sparse Core Ops, SparseCore 0:
  62.4 21.7 all-reduce.1
where the time goes:
time: 119 us; the launch traced here: 118 us
  waiting for transfers between devices  37.1 us (31%)
  blocking collectives  22.6 us (19%)
  starting transfers between devices  18.2 us (15%)
  matrix products  16 us (13%)
  between operations  13.6 us (11%)
  other arithmetic  8.02 us (7%)
  local copies, waits for them, and re-layouts  2.73 us (2%)
    psum x1, waiting for transfers between devices, shards(): summed = lax.psum(part_sum, 'chan')  21.2 us
    all_to_all x1, blocking collectives, shards(): lax.all_to_all(back_rows, ('locus', 'design'), split_axis=0, concat_axis=...  20.5 us
    all_to_all x1, starting transfers between devices, shards(): lax.all_to_all(send_slots, ('locus', 'design'), split_axis=0, concat_axis...  7.25 us
    all_to_all x1, waiting for transfers between devices, shards(): lax.all_to_all(send_rows, ('locus', 'design'), split_axis=0, concat_axis=...  5.68 us
    ppermute x2, waiting for transfers between devices, with_halo(): lax.ppermute(head, axis, [((i + 1) % count, i) for i in range(ends)])  5.54 us
    ppermute x2, starting transfers between devices, with_halo(): lax.ppermute(tail, axis, [(i, (i + 1) % count) for i in range(ends)])  4.95 us
    dot_general x3, matrix products, shards(): lax.dot_general(padded_gradient[lower_boundary:lower_boundary + bins_per_...  4.77 us
    all_to_all x1, waiting for transfers between devices, shards(): lax.all_to_all(send_slots, ('locus', 'design'), split_axis=0, concat_axis...  4.64 us
  transfers between devices with their start and end apart: 7, of which 5 were waited for; matrix products, arithmetic and copies ran while one was open for 5% of the time, Pallas kernels for 0%

commit v1 on v0

--- a/solution.py
+++ b/solution.py
@@ -4,6 +4,29 @@
 from jax.sharding import PartitionSpec as P
 
 DILATION_STEP = 32
+
+
+def split_up(shard, dim, length):
+    shape = shard.shape
+    blocks = shard.reshape(*shape[:dim], length, shape[dim] // length, *shape[dim + 1 :])
+    return jnp.moveaxis(blocks, dim, 0)
+
+
+def in_order(tiles, dim):
+    tiles = jnp.moveaxis(tiles, 0, dim)
+    dims = tiles.shape
+    return tiles.reshape(*dims[:dim], dims[dim] * dims[dim + 1], *dims[dim + 2 :])
+
+
+def rotated_exchange(x, axis, split_dim, concat_dim):
+    length, index = (lax.axis_size(axis), lax.axis_index(axis))
+    blocks = split_up(x, split_dim, length)
+    outs = [blocks[index]]
+    for turn in range(1, length):
+        sent = blocks[(index + turn) % length]
+        outs.append(lax.ppermute(sent, axis, [(i, (i + turn) % length) for i in range(length)]))
+    blocks = jnp.stack(outs)[(index - jnp.arange(length)) % length]
+    return in_order(blocks, concat_dim)
 
 
 def with_halo(cells, sides, width):
@@ -64,7 +87,7 @@
     ).astype(jnp.bfloat16)
     send_slots = jnp.sum(jnp.where(placer, slot_ids[None, :], 0), axis=1)
     recv_rows, recv_slots = (
-        lax.all_to_all(send_rows, ("locus", "design"), split_axis=0, concat_axis=0, tiled=True),
+        rotated_exchange(send_rows, ("locus", "design"), 0, 0),
         lax.all_to_all(send_slots, ("locus", "design"), split_axis=0, concat_axis=0, tiled=True),
     )
     chooser = recv_slots[:, None] == jnp.arange(slots_dev, dtype=jnp.int32)[None, :]

time: 119 us -> 127 us (1.067)
  starting transfers between devices: 18.2 us -> 23.2 us
  waiting for transfers between devices: 37.1 us -> 40.2 us
    ppermute x0 -> x7, waiting for transfers between devices: none -> 14.2 us  [rotated_exchange(): lax.ppermute(sent, axis, [(i, (i + turn) % length) for i in range(length)])]
    ppermute x0 -> x7, starting transfers between devices: none -> 9.59 us  [rotated_exchange(): lax.ppermute(sent, axis, [(i, (i + turn) % length) for i in range(length)])]
    all_to_all x1 -> x0, waiting for transfers between devices: 5.68 us -> none  [shards(): lax.all_to_all(send_rows, ('locus', 'design'), split_axis=0, concat_axis=...]
    all_to_all x1, waiting for transfers between devices: 4.64 us -> 0.01 us  [shards(): lax.all_to_all(send_slots, ('locus', 'design'), split_axis=0, concat_axis...]
    all_to_all x1 -> x0, starting transfers between devices: 3.41 us -> none  [shards(): lax.all_to_all(send_rows, ('locus', 'design'), split_axis=0, concat_axis=...]
  transfers between devices with their start and end apart: 7 -> 13, of which waited for: 5 -> 6; matrix products, arithmetic and copies ran while one was open for 5% -> 4% of each run, Pallas kernels for 0% -> 0%
where the time goes in v1:
time: 127 us; the launch traced here: 126 us
  waiting for transfers between devices  40.2 us (32%)
  starting transfers between devices  23.2 us (18%)
  blocking collectives  22.6 us (18%)
  matrix products  15.3 us (12%)
  between operations  13.8 us (11%)
  other arithmetic  8.05 us (6%)
  local copies, waits for them, and re-layouts  3.34 us (3%)
    all_to_all x1, blocking collectives, shards(): lax.all_to_all(back_rows, ('locus', 'design'), split_axis=0, concat_axis=...  20.5 us
    psum x1, waiting for transfers between devices, shards(): summed = lax.psum(part_sum, 'chan')  20.4 us
    ppermute x7, waiting for transfers between devices, rotated_exchange(): lax.ppermute(sent, axis, [(i, (i + turn) % length) for i in range(length)])  14.2 us
    ppermute x7, starting transfers between devices, rotated_exchange(): lax.ppermute(sent, axis, [(i, (i + turn) % length) for i in range(length)])  9.59 us
    all_to_all x1, starting transfers between devices, shards(): lax.all_to_all(send_slots, ('locus', 'design'), split_axis=0, concat_axis...  7.25 us
    ppermute x2, waiting for transfers between devices, with_halo(): lax.ppermute(head, axis, [((i + 1) % count, i) for i in range(ends)])  5.54 us
    dot_general x3, matrix products, shards(): lax.dot_general(padded_gradient[lower_boundary:lower_boundary + bins_per_...  4.74 us
    add_any x1, other arithmetic, gelu_pull(): jax.nn.gelu(argument, approximate=True)  4.06 us
  transfers between devices with their start and end apart: 13, of which 6 were waited for; matrix products, arithmetic and copies ran while one was open for 4% of the time, Pallas kernels for 0%

profile of v1, /device:TPU:0, one launch (start us, length us, event | category | flops | bytes accessed | tf_op | source)
XLA Modules:
  0.0 126.5 jit_solution(15950553616746433226)
XLA Ops:
  6.5 0.8 fusion.66
  7.6 0.8 select_reduce_fusion.1
  8.4 0.7 multiply_add_fusion
  9.1 0.8 select_reduce_fusion
  9.8 0.7 all_to_all.14
  10.5 7.3 %all-to-all-start = ((s32[8,32,1]{1,2,0:T(1,128)}), s32[8,32,1]{1,2,0:T(1,128)S(1)}, u32[]{:S(2)}, u32[]{:S(2)}) async-start(s32[8,32,1]{1,2,0:T(1,128)} %all_to_all.14), calls=%async_computation | async-start | bytes 8192 | tf_op jit(solution)/shard_map/all_to_all | solution.py:91
  17.9 1.1 convolution_convert_fusion
  19.1 4.6 %collective-permute-start.6 = (bf16[32,512]{1,0:T(8,128)(2,1)S(1)}, bf16[32,512]{1,0:T(8,128)(2,1)S(1)}, u32[]{:S(2)}, u32[]{:S(2)}) collective-permute-start(bf16[32,512]{1,0:T(8,128)(2,1)S(1)} %get-tuple-element.7), channel_id=1, source_target_pairs={{0,14},{2,0},{4,2},{6,4},{8,6},{10,8},{12,10},{14,12},{1,15},{3,1}... | collective-permute-start | bytes 98312 | tf_op jit(solution)/shard_map/ppermute | solution.py:27
  24.3 2.9 %collective-permute-start.3 = (bf16[32,512]{1,0:T(8,128)(2,1)S(1)}, bf16[32,512]{1,0:T(8,128)(2,1)S(1)}, u32[]{:S(2)}, u32[]{:S(2)}) collective-permute-start(bf16[32,512]{1,0:T(8,128)(2,1)S(1)} %get-tuple-element.10), channel_id=1, source_target_pairs={{0,8},{2,10},{4,12},{6,14},{8,0},{10,2},{12,4},{14,6},{1,9},{3,11}... | collective-permute-start | bytes 98312 | tf_op jit(solution)/shard_map/ppermute | solution.py:27
  27.2 1.5 %collective-permute-start = (bf16[32,512]{1,0:T(8,128)(2,1)S(1)}, bf16[32,512]{1,0:T(8,128)(2,1)S(1)}, u32[]{:S(2)}, u32[]{:S(2)}) collective-permute-start(bf16[32,512]{1,0:T(8,128)(2,1)S(1)} %get-tuple-element.13), channel_id=1, source_target_pairs={{0,2},{2,4},{4,6},{6,8},{8,10},{10,12},{12,14},{14,0},{1,3},{3,5},... | collective-permute-start | bytes 98312 | tf_op jit(solution)/shard_map/ppermute | solution.py:27
  28.7 0.7 reshape.115
  31.2 2.8 %collective-permute-done = bf16[32,512]{1,0:T(8,128)(2,1)S(1)} collective-permute-done((bf16[32,512]{1,0:T(8,128)(2,1)S(1)}, bf16[32,512]{1,0:T(8,128)(2,1)S(1)}, u32[]{:S(2)}, u32[]{:S(2)}) %collective-permute-start) | collective-permute-done | bytes 32800 | tf_op jit(solution)/shard_map/ppermute | solution.py:27
  34.0 5.7 %collective-permute-done.1 = bf16[32,512]{1,0:T(8,128)(2,1)S(1)} collective-permute-done((bf16[32,512]{1,0:T(8,128)(2,1)S(1)}, bf16[32,512]{1,0:T(8,128)(2,1)S(1)}, u32[]{:S(2)}, u32[]{:S(2)}) %collective-permute-start.1) | collective-permute-done | bytes 32800 | tf_op jit(solution)/shard_map/ppermute | solution.py:27
  39.7 5.7 %collective-permute-done.2 = bf16[32,512]{1,0:T(8,128)(2,1)S(1)} collective-permute-done((bf16[32,512]{1,0:T(8,128)(2,1)S(1)}, bf16[32,512]{1,0:T(8,128)(2,1)S(1)}, u32[]{:S(2)}, u32[]{:S(2)}) %collective-permute-start.2) | collective-permute-done | bytes 32800 | tf_op jit(solution)/shard_map/ppermute | solution.py:27
  46.4 1.3 %collective-permute-start.7 = (bf16[32,128]{1,0:T(8,128)(2,1)S(1)}, bf16[32,128]{1,0:T(8,128)(2,1)S(1)}, u32[]{:S(2)}, u32[]{:S(2)}) collective-permute-start(bf16[32,128]{1,0:T(8,128)(2,1)S(1)} %get-tuple-element.15), channel_id=1, source_target_pairs={{0,4},{4,8},{8,12},{1,5},{5,9},{9,13},{2,6},{6,10},{10,14},{3,7},{... | collective-permute-start | bytes 24584 | tf_op jit(solution)/shard_map/ppermute | solution.py:40
  47.7 1.3 %collective-permute-start.8 = (bf16[32,128]{1,0:T(8,128)(2,1)S(1)}, bf16[32,128]{1,0:T(8,128)(2,1)S(1)}, u32[]{:S(2)}, u32[]{:S(2)}) collective-permute-start(bf16[32,128]{1,0:T(8,128)(2,1)S(1)} %get-tuple-element.16), channel_id=1, source_target_pairs={{4,0},{8,4},{12,8},{5,1},{9,5},{13,9},{6,2},{10,6},{14,10},{7,3},{... | collective-permute-start | bytes 24584 | tf_op jit(solution)/shard_map/ppermute | solution.py:42
  49.0 2.1 %all_gather.3 = bf16[128,1536]{1,0:T(8,128)(2,1)S(1)} all-gather(bf16[128,768]{1,0:T(8,128)(2,1)S(1)} %copy-done.2), channel_id=1, replica_groups=mesh['groups'=2,'locus'=4,'design'=2,'chan'=2] {'chan'}, dimensions={1}, use_global_device_ids=true | all-gather | bytes 589824 | tf_op jit(solution)/shard_map/all_gather | solution.py:104
  51.1 2.1 %collective-permute-done.8 = bf16[32,128]{1,0:T(8,128)(2,1)S(1)} collective-permute-done((bf16[32,128]{1,0:T(8,128)(2,1)S(1)}, bf16[32,128]{1,0:T(8,128)(2,1)S(1)}, u32[]{:S(2)}, u32[]{:S(2)}) %collective-permute-start.8) | collective-permute-done | bytes 8224 | tf_op jit(solution)/shard_map/ppermute | solution.py:42
  53.3 2.9 %fusion.7 = (bf16[576,1536]{1,0:T(8,128)(2,1)S(1)}, f32[576,1536]{1,0:T(8,128)}) fusion(bf16[128,1536]{1,0:T(8,128)(2,1)S(1)} %all_gather.3, bf16[32,128]{1,0:T(8,128)(2,1)S(1)} %collective-permute-done.8, bf16[512,128]{1,0:T(8,128)(2,1)S(1)} %fusion.50, bf16[32,128]{1,0:T(8,128)(2,1)S(1)} %collective-permute-done.7), kind=kOutput, calls=%fused_computation.11 | convolution fusion | flops 234897408 | bytes 5849088 | tf_op jit(solution)/shard_map/dot_general | solution.py:105
  56.2 1.0 fusion.18
  57.2 1.0 fusion.22
  58.2 1.2 multiply_convert_fusion
  59.4 2.4 %collective-permute-start.10 = (bf16[32,384]{1,0:T(8,128)(2,1)S(1)}, bf16[32,384]{1,0:T(8,128)(2,1)S(1)}, u32[]{:S(2)}, u32[]{:S(2)}) collective-permute-start(bf16[32,384]{1,0:T(8,128)(2,1)S(1)} %get-tuple-element.6), channel_id=1, source_target_pairs={{0,4},{4,8},{8,12},{1,5},{5,9},{9,13},{2,6},{6,10},{10,14},{3,7},{... | collective-permute-start | bytes 73736 | tf_op jit(solution)/shard_map/ppermute | solution.py:40
  61.8 1.0 fusion.31
  62.8 1.3 %collective-permute-start.9 = (bf16[32,384]{1,0:T(8,128)(2,1)S(1)}, bf16[32,384]{1,0:T(8,128)(2,1)S(1)}, u32[]{:S(2)}, u32[]{:S(2)}) collective-permute-start(bf16[32,384]{1,0:T(8,128)(2,1)S(1)} %get-tuple-element.5), channel_id=1, source_target_pairs={{4,0},{8,4},{12,8},{5,1},{9,5},{13,9},{6,2},{10,6},{14,10},{7,3},{... | collective-permute-start | bytes 73736 | tf_op jit(solution)/shard_map/ppermute | solution.py:42
  64.1 1.0 fusion.28
  65.1 3.4 %collective-permute-done.9 = bf16[32,384]{1,0:T(8,128)(2,1)S(1)} collective-permute-done((bf16[32,384]{1,0:T(8,128)(2,1)S(1)}, bf16[32,384]{1,0:T(8,128)(2,1)S(1)}, u32[]{:S(2)}, u32[]{:S(2)}) %collective-permute-start.9) | collective-permute-done | bytes 24608 | tf_op jit(solution)/shard_map/ppermute | solution.py:42
  68.5 2.7 %fusion.8 = f32[512,1536]{1,0:T(8,128)} fusion(f32[512,1536]{1,0:T(8,128)S(1)} %fusion.28, f32[512,1536]{1,0:T(8,128)S(1)} %fusion.31, bf16[3,1536,384]{2,1,0:T(8,128)(2,1)S(1)} %copy-done.1, bf16[32,384]{1,0:T(8,128)(2,1)S(1)} %collective-permute-done.9, bf16[512,384]{1,0:T(8,128)(2,1)S(1)} %multiply_convert_fusion), kind=kOutput, calls=%fused_computation.13 | convolution fusion | flops 606339072 | bytes 11034624 | tf_op jit(solution)/shard_map/dot_general | solution.py:121
  71.9 20.4 %all-reduce.2.cloned.1.call-done = f32[512,1536]{1,0:T(8,128)} async-done(((f32[512,1536]{1,0:T(8,128)}), f32[512,1536]{1,0:T(8,128)}) %all-reduce.2.cloned.1.call-update) | async-done | bytes 3145744 | tf_op jit(solution)/shard_map/psum | solution.py:128
  92.3 4.1 %fusion.14 = f32[512,1536]{1,0:T(8,128)S(1)} fusion(f32[576,1536]{1,0:T(8,128)} %get-tuple-element.18, f32[512,1536]{1,0:T(8,128)} %all-reduce.2.cloned.1.call-done, f32[1536]{0:T(1024)S(1)} %convert_element_type.38), kind=kLoop, calls=%fused_computation.19 | loop fusion | flops 15728640 | bytes 9443328 | tf_op jit(solution)/shard_map/transpose(jvp())/add_any | solution.py:55
  98.0 20.5 %all_to_all.21 = f32[8,32,512]{2,1,0:T(8,128)S(1)} all-to-all(f32[8,32,512]{2,1,0:T(8,128)S(1)} %fusion.59), channel_id=1, replica_groups=mesh['groups'=2,'locus'=4,'design'=2,'chan'=2] {'locus','design'}, dimensions={0} | all-to-all | bytes 1048576 | tf_op jit(solution)/shard_map/all_to_all | solution.py:134
  118.5 1.1 fusion.57
  (49 shorter events, 5.8 us)
Async XLA Ops:
  6.5 22.9 %copy-start = (bf16[384,1536]{1,0:T(8,128)(2,1)S(1)}, bf16[384,1536]{1,0:T(8,128)(2,1)}, u32[]{:S(2)}) copy-start(bf16[384,1536]{1,0:T(8,128)(2,1)} %param.14) | copy-start | bytes 3538948
  6.5 39.8 %copy-start.3 = (bf16[1,512,128]{2,1,0:T(8,128)(2,1)S(1)}, bf16[1,512,128]{2,1,0:T(8,128)(2,1)}, u32[]{:S(2)}) copy-start(bf16[1,512,128]{2,1,0:T(8,128)(2,1)} %param.8) | copy-start | bytes 393220
  6.5 42.5 %copy-start.2 = (bf16[128,768]{1,0:T(8,128)(2,1)S(1)}, bf16[128,768]{1,0:T(8,128)(2,1)}, u32[]{:S(2)}) copy-start(bf16[128,768]{1,0:T(8,128)(2,1)} %param.12) | copy-start | bytes 589828
  10.5 19.4 %all-to-all-start = ((s32[8,32,1]{1,2,0:T(1,128)}), s32[8,32,1]{1,2,0:T(1,128)S(1)}, u32[]{:S(2)}, u32[]{:S(2)}) async-start(s32[8,32,1]{1,2,0:T(1,128)} %all_to_all.14), calls=%async_computation | async-start | bytes 8192 | tf_op jit(solution)/shard_map/all_to_all | solution.py:91
  17.8 74.6 %all-reduce.2.cloned.1.call-start = ((), (), s32[]{:S(2)}) async-start(), calls=%async_computation.2 | async-start | bytes 6291456 | tf_op jit(solution)/shard_map/psum | solution.py:128
  19.1 26.3 %collective-permute-start.6 = (bf16[32,512]{1,0:T(8,128)(2,1)S(1)}, bf16[32,512]{1,0:T(8,128)(2,1)S(1)}, u32[]{:S(2)}, u32[]{:S(2)}) collective-permute-start(bf16[32,512]{1,0:T(8,128)(2,1)S(1)} %get-tuple-element.7), channel_id=1, source_target_pairs={{0,14},{2,0},{4,2},{6,4},{8,6},{10,8},{12,10},{14,12},{1,15},{3,1}... | collective-permute-start | bytes 98312 | tf_op jit(solution)/shard_map/ppermute | solution.py:27
  23.8 21.7 %collective-permute-start.5 = (bf16[32,512]{1,0:T(8,128)(2,1)S(1)}, bf16[32,512]{1,0:T(8,128)(2,1)S(1)}, u32[]{:S(2)}, u32[]{:S(2)}) collective-permute-start(bf16[32,512]{1,0:T(8,128)(2,1)S(1)} %get-tuple-element.8), channel_id=1, source_target_pairs={{0,12},{2,14},{4,0},{6,2},{8,4},{10,6},{12,8},{14,10},{1,13},{3,15... | collective-permute-start | bytes 98312 | tf_op jit(solution)/shard_map/ppermute | solution.py:27
  24.3 21.1 %collective-permute-start.4 = (bf16[32,512]{1,0:T(8,128)(2,1)S(1)}, bf16[32,512]{1,0:T(8,128)(2,1)S(1)}, u32[]{:S(2)}, u32[]{:S(2)}) collective-permute-start(bf16[32,512]{1,0:T(8,128)(2,1)S(1)} %get-tuple-element.9), channel_id=1, source_target_pairs={{0,10},{2,12},{4,14},{6,0},{8,2},{10,4},{12,6},{14,8},{1,11},{3,13... | collective-permute-start | bytes 98312 | tf_op jit(solution)/shard_map/ppermute | solution.py:27
  24.3 21.1 %collective-permute-start.3 = (bf16[32,512]{1,0:T(8,128)(2,1)S(1)}, bf16[32,512]{1,0:T(8,128)(2,1)S(1)}, u32[]{:S(2)}, u32[]{:S(2)}) collective-permute-start(bf16[32,512]{1,0:T(8,128)(2,1)S(1)} %get-tuple-element.10), channel_id=1, source_target_pairs={{0,8},{2,10},{4,12},{6,14},{8,0},{10,2},{12,4},{14,6},{1,9},{3,11}... | collective-permute-start | bytes 98312 | tf_op jit(solution)/shard_map/ppermute | solution.py:27
  27.2 6.7 %collective-permute-start = (bf16[32,512]{1,0:T(8,128)(2,1)S(1)}, bf16[32,512]{1,0:T(8,128)(2,1)S(1)}, u32[]{:S(2)}, u32[]{:S(2)}) collective-permute-start(bf16[32,512]{1,0:T(8,128)(2,1)S(1)} %get-tuple-element.13), channel_id=1, source_target_pairs={{0,2},{2,4},{4,6},{6,8},{8,10},{10,12},{12,14},{14,0},{1,3},{3,5},... | collective-permute-start | bytes 98312 | tf_op jit(solution)/shard_map/ppermute | solution.py:27
  34.0 5.7 %collective-permute-start.1 = (bf16[32,512]{1,0:T(8,128)(2,1)S(1)}, bf16[32,512]{1,0:T(8,128)(2,1)S(1)}, u32[]{:S(2)}, u32[]{:S(2)}) collective-permute-start(bf16[32,512]{1,0:T(8,128)(2,1)S(1)} %get-tuple-element.12), channel_id=1, source_target_pairs={{0,4},{2,6},{4,8},{6,10},{8,12},{10,14},{12,0},{14,2},{1,5},{3,7},... | collective-permute-start | bytes 98312 | tf_op jit(solution)/shard_map/ppermute | solution.py:27
  39.7 5.7 %collective-permute-start.2 = (bf16[32,512]{1,0:T(8,128)(2,1)S(1)}, bf16[32,512]{1,0:T(8,128)(2,1)S(1)}, u32[]{:S(2)}, u32[]{:S(2)}) collective-permute-start(bf16[32,512]{1,0:T(8,128)(2,1)S(1)} %get-tuple-element.11), channel_id=1, source_target_pairs={{0,6},{2,8},{4,10},{6,12},{8,14},{10,0},{12,2},{14,4},{1,7},{3,9},... | collective-permute-start | bytes 98312 | tf_op jit(solution)/shard_map/ppermute | solution.py:27
  46.4 4.7 %collective-permute-start.7 = (bf16[32,128]{1,0:T(8,128)(2,1)S(1)}, bf16[32,128]{1,0:T(8,128)(2,1)S(1)}, u32[]{:S(2)}, u32[]{:S(2)}) collective-permute-start(bf16[32,128]{1,0:T(8,128)(2,1)S(1)} %get-tuple-element.15), channel_id=1, source_target_pairs={{0,4},{4,8},{8,12},{1,5},{5,9},{9,13},{2,6},{6,10},{10,14},{3,7},{... | collective-permute-start | bytes 24584 | tf_op jit(solution)/shard_map/ppermute | solution.py:40
  47.7 5.5 %collective-permute-start.8 = (bf16[32,128]{1,0:T(8,128)(2,1)S(1)}, bf16[32,128]{1,0:T(8,128)(2,1)S(1)}, u32[]{:S(2)}, u32[]{:S(2)}) collective-permute-start(bf16[32,128]{1,0:T(8,128)(2,1)S(1)} %get-tuple-element.16), channel_id=1, source_target_pairs={{4,0},{8,4},{12,8},{5,1},{9,5},{13,9},{6,2},{10,6},{14,10},{7,3},{... | collective-permute-start | bytes 24584 | tf_op jit(solution)/shard_map/ppermute | solution.py:42
  51.1 5.1 %copy-start.1 = (bf16[3,1536,384]{2,1,0:T(8,128)(2,1)S(1)}, bf16[3,1536,384]{2,1,0:T(8,128)(2,1)}, u32[]{:S(2)}) copy-start(bf16[3,1536,384]{2,1,0:T(8,128)(2,1)} %param.13) | copy-start | bytes 10616836
  59.4 4.7 %collective-permute-start.10 = (bf16[32,384]{1,0:T(8,128)(2,1)S(1)}, bf16[32,384]{1,0:T(8,128)(2,1)S(1)}, u32[]{:S(2)}, u32[]{:S(2)}) collective-permute-start(bf16[32,384]{1,0:T(8,128)(2,1)S(1)} %get-tuple-element.6), channel_id=1, source_target_pairs={{0,4},{4,8},{8,12},{1,5},{5,9},{9,13},{2,6},{6,10},{10,14},{3,7},{... | collective-permute-start | bytes 73736 | tf_op jit(solution)/shard_map/ppermute | solution.py:40
  62.8 5.7 %collective-permute-start.9 = (bf16[32,384]{1,0:T(8,128)(2,1)S(1)}, bf16[32,384]{1,0:T(8,128)(2,1)S(1)}, u32[]{:S(2)}, u32[]{:S(2)}) collective-permute-start(bf16[32,384]{1,0:T(8,128)(2,1)S(1)} %get-tuple-element.5), channel_id=1, source_target_pairs={{4,0},{8,4},{12,8},{5,1},{9,5},{13,9},{6,2},{10,6},{14,10},{7,3},{... | collective-permute-start | bytes 73736 | tf_op jit(solution)/shard_map/ppermute | solution.py:42
  71.3 0.7 copy-start.4
Sparse Core Ops, SparseCore 0:
  71.4 20.8 all-reduce.1
